TPU v7x, 512 devices: a whole 4x4x16 slice. The times are simulated.
512 devices in a mesh: ctx: 64 (over z_lo, y, core), tp: 8 (over x, z_hi).
Axes of the slice: x: 4, y: 4, z: 16 (z_hi: 2, z_lo: 8; z = z_hi * 8 + z_lo), core: 2. Of those that a mesh axis runs over, the one named last changes fastest.
Arguments:
- queries: bfloat16 [4, 64, 8192], P(None, 'ctx', 'tp'), may hold values from -15 to 15
- cache_keys: bfloat16 [4, 131072, 1024], P(None, 'ctx', 'tp'), may hold values from -6 to 6
- cache_values: bfloat16 [4, 131072, 1024], P(None, 'ctx', 'tp'), may hold values from -6 to 6
- new_keys: bfloat16 [4, 64, 1024], P(None, 'ctx', 'tp'), may hold values from -6 to 6
- new_values: bfloat16 [4, 64, 1024], P(None, 'ctx', 'tp'), may hold values from -6 to 6
- out_weight: bfloat16 [8192, 8192], P('tp', 'ctx'), may hold values from -0.0625 to 0.0625
Outputs:
- projected: bfloat16 [4, 64, 8192], P(None, 'tp', 'ctx')
All inputs are finite; a program needn't handle non-finite values.
Results may differ from a plain program's by a relative error of at most 0.017.
Values may be sent and summed in bfloat16 or wider, within the bound.
A program may use at most 192 MiB of HBM per device.

v0:
```python
import math

import jax
import jax.numpy as jnp
from jax import lax
from jax.sharding import PartitionSpec as P

HD = 128


def local(queries, cache_keys, cache_values, new_keys, new_values, out_weight):
    gathered = lax.all_gather(queries, "ctx", axis=1, tiled=True)
    seq_count, total_new, query_cols = gathered.shape
    own_new = new_keys.shape[1]
    kv_local = cache_keys.shape[2] // HD
    heads_local = query_cols // HD
    per_group = heads_local // kv_local
    inv_root = 1.0 / math.sqrt(HD)
    first_pos = lax.axis_index("ctx") * own_new
    key_pos = first_pos + jnp.arange(own_new, dtype=jnp.int32)
    visible = key_pos[None, :] <= jnp.arange(total_new, dtype=jnp.int32)[:, None]

    def attend_one(inputs_one):
        query_one, keys_one, values_one, newk_one, newv_one = inputs_one
        query_heads = query_one.reshape(total_new, kv_local, per_group, HD)
        key_heads = keys_one.reshape(-1, kv_local, HD)
        value_heads = values_one.reshape(-1, kv_local, HD)
        newk_heads = newk_one.reshape(own_new, kv_local, HD)
        newv_heads = newv_one.reshape(own_new, kv_local, HD)
        scores = (
            jnp.einsum("tkgd,skd->tkgs", query_heads, key_heads, preferred_element_type=jnp.float32)
            * inv_root
        )
        fresh_scores = (
            jnp.einsum(
                "tkgd,skd->tkgs", query_heads, newk_heads, preferred_element_type=jnp.float32
            )
            * inv_root
        )
        fresh_scores = jnp.where(visible[:, None, None, :], fresh_scores, -jnp.inf)
        row_peak = jnp.maximum(jnp.max(scores, axis=-1), jnp.max(fresh_scores, axis=-1))
        old_weights = jnp.exp(scores - row_peak[..., None])
        new_weights = jnp.exp(fresh_scores - row_peak[..., None])
        weight_sum = jnp.sum(old_weights, axis=-1) + jnp.sum(new_weights, axis=-1)
        numerator = jnp.einsum(
            "tkgs,skd->tkgd",
            old_weights.astype(jnp.bfloat16),
            value_heads,
            preferred_element_type=jnp.float32,
        )
        numerator = numerator + jnp.einsum(
            "tkgs,skd->tkgd",
            new_weights.astype(jnp.bfloat16),
            newv_heads,
            preferred_element_type=jnp.float32,
        )
        return (
            row_peak.reshape(total_new, heads_local),
            weight_sum.reshape(total_new, heads_local),
            numerator.reshape(total_new, heads_local, HD),
        )

    row_peak, weight_sum, numerator = lax.map(
        attend_one, (gathered, cache_keys, cache_values, new_keys, new_values)
    )
    global_peak = lax.pmax(row_peak, "ctx")
    factor = jnp.exp(row_peak - global_peak)
    share_numer, share_sum = (
        lax.psum_scatter(numerator * factor[..., None], "ctx", scatter_dimension=1, tiled=True),
        lax.psum_scatter(weight_sum * factor, "ctx", scatter_dimension=1, tiled=True),
    )
    attended = (
        (share_numer / share_sum[..., None])
        .reshape(seq_count, own_new, query_cols)
        .astype(jnp.bfloat16)
    )
    partial_out = jnp.einsum(
        "snq,qd->snd",
        lax.all_gather(attended, "ctx", axis=1, tiled=True),
        out_weight,
        preferred_element_type=jnp.float32,
    )
    return lax.psum_scatter(partial_out.astype(jnp.bfloat16), "tp", scatter_dimension=1, tiled=True)


def solution(mesh):
    return jax.shard_map(
        local,
        mesh=mesh,
        in_specs=(
            P(None, "ctx", "tp"),
            P(None, "ctx", "tp"),
            P(None, "ctx", "tp"),
            P(None, "ctx", "tp"),
            P(None, "ctx", "tp"),
            P("tp", "ctx"),
        ),
        out_specs=P(None, "tp", "ctx"),
        check_vma=False,
    )
```

profile of v0, /device:TPU:7, one launch (start us, length us, event | category | flops | bytes accessed | tf_op | source)
XLA Modules:
  0.0 1247.5 jit_solution(8344609494232487610)
XLA Ops:
  6.5 128.0 %all_gather.6 = bf16[4,64,1024]{2,0,1:T(4,128)(2,1)S(1)} all-gather(bf16[4,1,1024]{2,0,1:T(4,128)(2,1)} %param.8), channel_id=1, replica_groups=mesh['ctx'=64,'tp'=8] {'ctx'}, dimensions={1}, use_global_device_ids=true | all-gather | bytes 532480 | tf_op jit(solution)/shard_map/all_gather | solution.py:12
  134.7 40.3 %while.15 = (s32[]{:T(128)}, f32[4,64,8]{1,2,0:T(8,128)S(1)}, f32[4,64,8]{1,2,0:T(8,128)S(1)}, f32[4,64,8,128]{3,2,0,1:T(8,128)S(1)}, bf16[4,2048,128]{2,1,0:T(8...) while((s32[]{:T(128)}, f32[4,64,8]{1,2,0:T(8,128)S(1)}, ...), condition=%wide.region_3.4_spmd.clone, body=%wide.region_0.3_spmd.clone.sunk | while | flops 545525952 | bytes 32037480 | solution.py:63
  134.8 3.7 bitcast_reduce_fusion.2
  138.5 0.7 fusion.49
  139.3 3.2 fusion.50
  142.7 1.9 fusion.52
  144.9 3.7 bitcast_reduce_fusion.2
  149.4 3.2 fusion.50
  152.8 1.9 fusion.52
  155.0 3.7 bitcast_reduce_fusion.2
  159.4 3.2 fusion.50
  162.9 1.9 fusion.52
  165.0 3.7 bitcast_reduce_fusion.2
  169.5 3.2 fusion.50
  172.9 1.9 fusion.52
  175.0 408.2 %pmax.7 = f32[4,64,8]{1,2,0:T(8,128)S(1)} all-reduce(f32[4,64,8]{1,2,0:T(8,128)S(1)} %get-tuple-element.60), channel_id=1, replica_groups=mesh['ctx'=64,'tp'=8] {'ctx'}, use_global_device_ids=true, to_apply=%region_4.5 | all-reduce | flops 2048 | bytes 16384 | tf_op jit(solution)/shard_map/pmax | solution.py:66
  583.3 1.3 broadcast_multiply_fusion
  584.9 1.3 dynamic-slice
  586.1 418.7 %all-reduce = f32[4,64,8]{2,0,1:T(4,128)S(1)} all-reduce(f32[4,64,8]{2,0,1:T(4,128)S(1)} %copy.29), channel_id=3, replica_groups=mesh['ctx'=64,'tp'=8] {'ctx'}, use_global_device_ids=true, to_apply=%region_6.7.clone | all-reduce | flops 2048 | bytes 16384
  1005.5 10.5 reduce-scatter.5.cloned.1.call-done
  1016.0 0.8 divide_convert_fusion
  1016.8 124.4 %all_gather.7 = bf16[4,64,1024]{2,0,1:T(4,128)(2,1)S(1)} all-gather(bf16[4,1,1024]{2,0,1:T(4,128)(2,1)S(1)} %convert_element_type.25), channel_id=1, replica_groups=mesh['ctx'=64,'tp'=8] {'ctx'}, dimensions={1}, use_global_device_ids=true | all-gather | bytes 532480 | tf_op jit(solution)/shard_map/all_gather | solution.py:79
  1142.2 97.1 %reduce-scatter.7.cloned.1.call-done = bf16[8,512]{1,0:T(8,128)(2,1)} async-done(((bf16[64,512]{1,0:T(8,128)(2,1)}), bf16[8,512]{1,0:T(8,128)(2,1)}) %reduce-scatter.7.cloned.1.call-update) | async-done | bytes 8208
  1239.3 0.7 reshape.132
  (78 shorter events, 7.0 us)
Async XLA Ops:
  6.5 1134.7 %copy-start = (bf16[1024,128]{1,0:T(8,128)(2,1)S(1)}, bf16[1024,128]{1,0:T(8,128)(2,1)}, u32[]{:S(2)}) copy-start(bf16[1024,128]{1,0:T(8,128)(2,1)} %param.13) | copy-start | bytes 786436
  6.5 1009.5 %reduce-scatter.5.cloned.1.call-start = ((), (), s32[]{:S(2)}) async-start(), calls=%async_computation.2 | async-start | bytes 1064960 | tf_op jit(solution)/shard_map/reduce_scatter | solution.py:69
  134.7 3.8 copy-start.2
  134.8 7.7 copy-start.3
  139.2 3.5 copy-start.1
  144.8 3.8 copy-start.2
  144.9 7.7 copy-start.3
  149.3 3.5 copy-start.1
  154.9 3.8 copy-start.2
  155.0 7.7 copy-start.3
  159.4 3.5 copy-start.1
  165.0 3.8 copy-start.2
  165.0 7.7 copy-start.3
  169.4 3.5 copy-start.1
  584.7 654.6 %reduce-scatter.7.cloned.1.call-start = ((), (), s32[]{:S(2)}) async-start(), calls=%async_computation.3 | async-start | bytes 73728
Sparse Core Ops, SparseCore 0:
  584.8 431.1 reduce-scatter.4
  1142.3 96.9 reduce-scatter.6
where the time goes:
time: 1250 us
  blocking collectives  1080 us (86%)
  waiting for transfers between devices  108 us (9%)
  matrix products  25.3 us (2%)
  other arithmetic  15.1 us (1%)
  between operations  13.5 us (1%)
    unnamed x1, blocking collectives  419 us
    pmax x1, blocking collectives, local(): global_peak = lax.pmax(row_peak, 'ctx')  408 us
    all_gather x1, blocking collectives, local(): gathered = lax.all_gather(queries, 'ctx', axis=1, tiled=True)  128 us
    all_gather x1, blocking collectives, local(): lax.all_gather(attended, 'ctx', axis=1, tiled=True)  124 us
    unnamed x3, waiting for transfers between devices  97.1 us
  transfers between devices with their start and end apart: 2, of which 2 were waited for; matrix products, arithmetic and copies ran while one was open for 0% of the time, Pallas kernels for 0%

commit v1 on v0

v1 whole, which is shorter than its diff:
```python
import functools
import math

import jax
import jax.numpy as jnp
from jax import lax
from jax.experimental import pallas as pl
from jax.experimental.pallas import tpu as pltpu
from jax.sharding import PartitionSpec as P

HD = 128
HEADS = 8
SEQS = 4
UNIT = SEQS * HEADS
PAD = 16
CHUNK = 256
SCALE = math.log2(math.e) / math.sqrt(HD)
MESH = pl.DeviceIdType.MESH
F32 = jnp.float32
BF16 = jnp.bfloat16


def iota(shape, dim):
    return lax.broadcasted_iota(jnp.int32, shape, dim)


def loop(first, last, body):
    lax.fori_loop(first, last, lambda i, c: (body(i), c)[1], 0)


def rounded(x):
    return x.astype(BF16).astype(F32)


def spread(packed, first):
    shape = (packed.shape[0], UNIT, HD)
    wide = jnp.broadcast_to(packed[:, None, :], shape)
    hit = iota(shape, 2) == iota(shape, 1) + first
    return jnp.sum(jnp.where(hit, wide, 0.0), axis=-1, keepdims=True)


def merge(stats, numers):
    peak = functools.reduce(jnp.maximum, stats)
    factors = [jnp.exp2(s - peak) for s in stats]
    total = sum((s + pltpu.roll(s, 96, 1)) * pltpu.roll(f, 64, 1) for s, f in zip(stats, factors))
    out = sum(n * spread(f, 0) for n, f in zip(numers, factors))
    return peak, total, out


def pack(peak, total):
    lead = rounded(total)
    rest = rounded(total - lead)
    lane = iota(peak.shape, 1)
    return jnp.where(lane < 64, peak, jnp.where(lane < 96, lead, pltpu.roll(rest, 32, 1)))


class Place:
    def __init__(self, sizes):
        self.Z, self.Y, self.C, self.T = sizes
        ctx = lax.axis_index("ctx")
        self.c = lax.rem(ctx, self.C)
        self.y = lax.rem(ctx // self.C, self.Y)
        self.z = ctx // (self.C * self.Y)
        self.ctx = ctx
        self.tp = lax.axis_index("tp")

    def z_at(self, k):
        return lax.rem(self.z + k + self.Z, self.Z)

    def y_at(self, k):
        return lax.rem(self.y + k + self.Y, self.Y)

    def tp_at(self, k):
        return lax.rem(self.tp + k + self.T, self.T)

    def ctx_of(self, z, y, c):
        return (z * self.Y + y) * self.C + c

    def copy(self, src, dst, send, recv, **axis):
        return pltpu.make_async_remote_copy(
            src_ref=src, dst_ref=dst, send_sem=send, recv_sem=recv, device_id=axis, device_id_type=MESH
        )


class Gather:
    def __init__(self, place, part, sems):
        self.p, self.part, self.H = place, part, place.Z // 2
        self.zz, self.ys, self.yr = sems
        self.half = place.z // self.H

    def z_copy(self, to, group):
        p = self.p
        block = self.part(p.y).at[p.z]
        return p.copy(block, block, self.zz.at[0, group], self.zz.at[1, group], ctx=p.ctx_of(to, p.y, p.c))

    def z_all(self, group):
        p = self.p
        block = self.part(p.y).at[pl.ds(0, self.H - 1 + group)]
        return p.copy(block, block, self.zz.at[0, group], self.zz.at[1, group], ctx=p.ctx_of(p.z_at(1), p.y, p.c))

    def half_at(self, group):
        return self.half if group == 0 else 1 - self.half

    def rows(self, group):
        return pl.ds(self.half_at(group) * self.H, self.H)

    def y_copy(self, k, group, send):
        p = self.p
        block = self.part(p.y if send else p.y_at(-k)).at[self.rows(group)]
        return p.copy(block, block, self.ys.at[group, k - 1], self.yr.at[group, k - 1], ctx=p.ctx_of(p.z, p.y_at(k), p.c))

    def start(self):
        H = self.H
        loop(0, H, lambda j: self.z_copy((1 - self.half) * H + lax.rem(self.p.z + j, H), 1).start())
        loop(1, H, lambda j: self.z_copy(self.half * H + lax.rem(self.p.z + j, H), 0).start())

    def along_y(self, group, order):
        if self.H - 1 + group:
            self.z_all(group).wait_recv()
        for k in order:
            self.y_copy(k, group, True).start()

    def arrived(self, k):
        for group in range(2):
            self.y_copy(k, group, False).wait_recv()

    def drain(self):
        for group in range(2):
            if self.H - 1 + group:
                self.z_all(group).wait_send()
            for k in range(1, self.p.Y):
                self.y_copy(k, group, True).wait_send()


def kernel(sizes, q_hbm, k_hbm, v_hbm, nk_hbm, nv_hbm, w_hbm, o_ref,
           kbuf, vbuf, vt, wbuf, qin, nkin, nvin, nkb, nvb, qrow, qbuf, qd, sbuf, pbuf, nb, st,
           ysb, yrb, zf, zsb, zss, zrb, zrs, abuf, af, pf, tf, ts, tr, of,
           ld, qsems, csems, asems, wsem, ry, rz, tt):
    p = Place(sizes)
    Z, Y, C, T = sizes
    z, y, c = p.z, p.y, p.c
    slots = C * Z
    rows = slots * HEADS
    near = [k for k in (1, 3, 2) if k < Y]
    units = [k for k in (2, 1, 3) if k < Y]

    def unit_at(i):
        return lax.rem(i, 2) * 2 + i // 2 if Y == 4 else i

    small = [pltpu.make_async_copy(a, b, ld.at[i]) for i, (a, b) in enumerate(((q_hbm, qin), (nk_hbm, nkin), (nv_hbm, nvin)))]
    w_load = pltpu.make_async_copy(w_hbm, wbuf.at[c], ld.at[3])

    def kv_load(s):
        return (pltpu.make_async_copy(k_hbm.at[s], kbuf.at[s], ld.at[4 + 2 * s]),
                pltpu.make_async_copy(v_hbm.at[s], vbuf.at[s], ld.at[5 + 2 * s]))

    for copy in small:
        copy.start()
    barrier = pltpu.get_barrier_semaphore()

    def greet(**axis):
        pl.semaphore_signal(barrier, inc=1, device_id=axis, device_id_type=MESH)

    def greet_tp(k):
        for cc in range(C):
            greet(ctx=p.ctx_of(z, y, cc), tp=p.tp_at(k))

    loop(1, Z, lambda k: greet(ctx=p.ctx_of(p.z_at(k), y, c)))
    for k in range(1, Y):
        for cc in range(C):
            greet(ctx=p.ctx_of(z, p.y_at(k), cc))
    greet(ctx=p.ctx_of(z, y, 1 - c))
    loop(1, T, greet_tp)
    for copy in [kv_load(s)[i] for i in (1, 0) for s in range(SEQS)]:
        copy.start()
    w_load.start()

    for copy in small:
        copy.wait()
    own = qin[...].astype(F32)
    for s in range(SEQS):
        for hd in range(HEADS):
            qrow[s * HEADS + hd:s * HEADS + hd + 1, :] = own[s:s + 1, hd * HD:(hd + 1) * HD]
    qbuf[y, c, z] = qrow[...].astype(BF16)
    qg = Gather(p, lambda yy: qbuf.at[yy, c], qsems)
    ag = Gather(p, lambda yy: abuf.at[yy], asems)
    pl.semaphore_wait(barrier, (Z - 1) + (Y * C - 1) + (T - 1) * C)
    qg.start()
    nk, nv = nkin[...].astype(F32), nvin[...].astype(F32)
    for s in range(SEQS):
        nkb[s] = jnp.broadcast_to(nk[s:s + 1], (PAD, HD)).astype(BF16)
        nvb[s] = jnp.broadcast_to(nv[s:s + 1], (8, HD))
    for pr in range(SEQS // 2):
        qd[pr] = jnp.zeros((2 * HD, 2 * rows), BF16)
        vt[pr, 2 * HD:, :] = jnp.ones((PAD, kbuf.shape[1]), BF16)

    def transpose(s):
        kv_load(s)[1].wait()
        at = pl.multiple_of(lax.rem(s, 2) * HD, HD)
        vt[s // 2, pl.ds(at, HD), :] = vbuf[s].T

    def attend(k):
        block = p.y_at(-k)
        x = qbuf[block].astype(F32).reshape(slots, SEQS, HEADS, HD)
        for s in range(SEQS):
            j = s % 2
            qd[s // 2, j * HD:(j + 1) * HD, j * rows:(j + 1) * rows] = x[:, s].reshape(rows, HD).T.astype(BF16)
        slot = lax.div(lax.rem(iota((8, 2 * rows), 1), rows), HEADS)
        token = lax.rem(slot, Z) * (Y * C) + block * C + lax.div(slot, Z)
        visible = token >= p.ctx
        chunk = min(CHUNK, kbuf.shape[1])
        chunks = [slice(a, a + chunk) for a in range(0, kbuf.shape[1], chunk)]

        def score(pr, at):
            keys = jnp.concatenate([kbuf[2 * pr, at], kbuf[2 * pr + 1, at]], axis=1)
            raw = jnp.dot(keys, qd[pr], preferred_element_type=F32)
            sbuf[pr, at] = raw
            return jnp.max(raw.reshape(chunk // 8, 8, 2 * rows), axis=0)

        def peak_of(pr, tops):
            keys = jnp.concatenate([nkb[2 * pr], nkb[2 * pr + 1]], axis=1)
            fresh = jnp.dot(keys, qd[pr], preferred_element_type=F32)[:8]
            fresh = jnp.where(visible, fresh, -jnp.inf)
            top = jnp.max(functools.reduce(jnp.maximum, tops + [fresh]), axis=0, keepdims=True)
            peak = rounded(top * SCALE)
            return peak, jnp.exp2(fresh * SCALE - peak)

        def weigh(pr, at, peak):
            pbuf[pr, at] = jnp.exp2(sbuf[pr, at] * SCALE - peak).astype(BF16)

        def finish(pr, peak, fresh):
            out = jnp.dot(vt[pr], pbuf[pr], preferred_element_type=F32)
            sub = iota((8, 2 * rows), 0)
            total = out[2 * HD:2 * HD + 8] + fresh
            three = jnp.where(sub == 0, peak, jnp.where(sub == 1, total, fresh))
            lane = iota((rows, HD), 1)
            row = iota((rows, HD), 0)
            for j in range(2):
                s = 2 * pr + j
                at = slice(j * rows, (j + 1) * rows)
                numer = out[j * HD:(j + 1) * HD, at].T
                cols = three[:, at].T
                numer = numer + rounded(cols[:, 2:3]) * nvb[s][:1]
                lead = rounded(cols[:, 1:2])
                rest = rounded(cols[:, 1:2] - lead)
                head = lax.rem(row, HEADS) + s * HEADS
                entry = jnp.where(lane == head, cols[:, 0:1], jnp.where(lane == head + 64, lead, jnp.where(lane == head + 96, rest, 0.0)))
                packed = jnp.sum(entry.reshape(slots, HEADS, HD), axis=1).reshape(C, Z, HD)
                st[k] = packed if s == 0 else st[k] + packed
                nb[k, :, :, s * HEADS:(s + 1) * HEADS, :] = numer.reshape(C, Z, HEADS, HD)

        tops = [score(0, at) for at in chunks]
        first = peak_of(0, tops)
        tops = []
        for at in chunks:
            tops.append(score(1, at))
            weigh(0, at, first[0])
        second = peak_of(1, tops)
        finish(0, *first)
        for at in chunks:
            weigh(1, at, second[0])
        finish(1, *second)

    def c_copy(k, group, send):
        block = qbuf.at[p.y_at(-k), c if send else 1 - c, qg.rows(group)]
        return p.copy(block, block, csems.at[0, group, k], csems.at[1, group, k], ctx=p.ctx_of(z, y, 1 - c))

    def w_copy():
        return p.copy(wbuf.at[c], wbuf.at[c], wsem.at[0], wsem.at[1], ctx=p.ctx_of(z, y, 1 - c))

    def core_at(j):
        return c if j == 0 else 1 - c

    def y_copy(k, j):
        dev = p.ctx_of(z, p.y_at(-k), core_at(j))
        return p.copy(ysb.at[k, j], yrb.at[k, j], ry.at[0, k, j], ry.at[1, k, j], ctx=dev)

    def z_copies(k):
        to = p.z_at(k)
        dev = p.ctx_of(to, y, c)
        return (p.copy(zsb.at[to], zrb.at[k - 1], rz.at[0, 0], rz.at[1, 0], ctx=dev),
                p.copy(zss.at[to], zrs.at[k - 1], rz.at[0, 1], rz.at[1, 1], ctx=dev))

    def z_all():
        dev = p.ctx_of(p.z_at(1), y, c)
        return (p.copy(zrb, zrb, rz.at[0, 0], rz.at[1, 0], ctx=dev), p.copy(zrs, zrs, rz.at[0, 1], rz.at[1, 1], ctx=dev))

    def t_copy(k, j):
        to = p.tp_at(k)
        return p.copy(ts.at[to * C + core_at(j)], tr.at[k * C + j], tt.at[0], tt.at[1], ctx=p.ctx_of(z, y, core_at(j)), tp=to)

    def t_all():
        block = tr.at[pl.ds(1, T * C - 1)]
        return p.copy(block, block, tt.at[0], tt.at[1], ctx=p.ctx_of(z, y, 1 - c))

    def message(stats, numer):
        pad = jnp.concatenate([stats, jnp.zeros((PAD - Z, HD), F32)], axis=0)
        return jnp.concatenate([numer.reshape(Z * UNIT, HD), pad], axis=0).astype(BF16)

    def reduce_y(k):
        ysb[k, 1] = message(st[k, 1 - c], nb[k, 1 - c])
        y_copy(k, 1).start()

        @pl.when(k > 0)
        def _():
            ysb[k, 0] = message(st[k, c], nb[k, c])
            y_copy(k, 0).start()

    def received(k, j):
        y_copy(k, j).wait_recv()
        got = yrb[k, j].astype(F32)
        return got[Z * UNIT:Z * UNIT + Z], got[:Z * UNIT].reshape(Z, UNIT, HD)

    def reduce_z():
        early = [(st[0, c], nb[0, c]), received(0, 1)] + [received(k, j) for k in units[:-1] for j in range(C)]
        peak, total, numer = merge(*zip(*early))
        late = [(pack(peak, total), numer)] + [received(units[-1], j) for j in range(C)]
        peak, total, numer = merge(*zip(*late))
        stats = pack(peak, total)
        zsb[...] = numer.astype(BF16)
        for k in range(Z):
            zss[k] = stats[k:k + 1]

        def send(k):
            for copy in z_copies(k):
                copy.start()
        loop(1, Z, send)
        zf[...] = numer

    def attended():
        stats, numers = [zss[z]], [zf[z][None]]
        for copy in z_all():
            copy.wait_recv()
        for k in range(Z - 1):
            stats.append(zrs[k])
            numers.append(zrb[k].astype(F32)[None])
        peak, total, numer = merge(stats, numers)
        abuf[y, z] = (numer / spread(total, 64))[0].astype(BF16)

    def project(k):
        block = p.y_at(-k)
        af[...] = abuf[block].reshape(Z * UNIT, HD).astype(F32)
        n = Z * SEQS
        heads = [af[pl.ds(hd, n, stride=HEADS), :].astype(BF16) for hd in range(HEADS)]
        at = pl.multiple_of(block * n, n)
        both = jnp.dot(jnp.concatenate(heads, axis=1), jnp.concatenate([wbuf[0], wbuf[1]], axis=1), preferred_element_type=F32)
        for cc in range(C):
            pf[cc, pl.ds(at, n), :] = both[:, cc * HD:(cc + 1) * HD]

    loop(0, SEQS // 2, transpose)
    for group in range(2):
        qg.along_y(group, units)
        c_copy(0, group, True).start()
    w_load.wait()
    w_copy().start()
    loop(SEQS // 2, SEQS, transpose)
    loop(0, SEQS, lambda s: kv_load(s)[0].wait())

    def unit(i):
        k = unit_at(i)
        for group in range(2):
            c_copy(k, group, False).wait_recv()
        attend(k)
        reduce_y(k)

        @pl.when(i == 0)
        def _():
            for k in near:
                qg.arrived(k)
                for group in range(2):
                    c_copy(k, group, True).start()

    loop(0, Y, unit)
    reduce_z()
    attended()
    ag.start()
    w_copy().wait_recv()
    for group in range(2):
        ag.along_y(group, units)
    for k in [0] + near:
        if k:
            ag.arrived(k)
        project(k)
    for t in range(T):
        for cc in range(C):
            tile = [pf[cc, pl.ds(SEQS * t + s, Y, stride=SEQS * Z), :] for s in range(SEQS)]
            tile = jnp.concatenate(tile, axis=0)
            tf[t * C + cc] = tile
            ts[t * C + cc] = tile.astype(BF16)

    def send(k):
        for j in range(C):
            t_copy(k, j).start()

    loop(1, T, send)
    t_copy(0, 1).start()
    mine = tf[p.tp * C + c]
    t_all().wait_recv()
    for k in range(1, T):
        mine = mine + tr[k * C].astype(F32)
    other = sum(tr[k * C + 1].astype(F32) for k in range(T))
    for s in range(SEQS):
        of[pl.ds(s * Y * C + c, Y, stride=C), :] = mine[s * Y:(s + 1) * Y]
        of[pl.ds(s * Y * C + 1 - c, Y, stride=C), :] = other[s * Y:(s + 1) * Y]
    o_ref[...] = of[...].astype(BF16)

    qg.drain()
    ag.drain()
    w_copy().wait_send()
    for k in range(Y):
        for group in range(2):
            c_copy(k, group, True).wait_send()
        for j in range(C):
            if k + j:
                y_copy(k, j).wait_send()
    for copy in z_all():
        copy.wait_send()
    t_all().wait_send()


def build(sizes, queries, keys, values, new_keys, new_values, weight):
    Z, Y, C, T = sizes
    S = keys.shape[1]
    V = pltpu.VMEM
    dma = pltpu.SemaphoreType.DMA
    slots = C * Z
    rows = slots * HEADS
    out_rows = SEQS * Y * C
    block = Z * UNIT + PAD
    tile = SEQS * Y
    scratch = [
        V((SEQS, S, HD), BF16), V((SEQS, S, HD), BF16), V((SEQS // 2, 2 * HD + PAD, S), BF16), V((C,) + weight.shape, BF16),
        V((SEQS, HEADS * HD), BF16), V((SEQS, HD), BF16), V((SEQS, HD), BF16),
        V((SEQS, PAD, HD), BF16), V((SEQS, 8, HD), F32), V((UNIT, HD), F32),
        V((Y, C, Z, UNIT, HD), BF16), V((SEQS // 2, 2 * HD, 2 * rows), BF16),
        V((SEQS // 2, S, 2 * rows), F32), V((SEQS // 2, S, 2 * rows), BF16),
        V((Y, C, Z, UNIT, HD), F32), V((Y, C, Z, HD), F32),
        V((Y, C, block, HD), BF16), V((Y, C, block, HD), BF16),
        V((Z, UNIT, HD), F32), V((Z, UNIT, HD), BF16), V((Z, 1, HD), F32),
        V((Z - 1, UNIT, HD), BF16), V((Z - 1, 1, HD), F32),
        V((Y, Z, UNIT, HD), BF16), V((Z * UNIT, HD), F32), V((C, Y * Z * SEQS, HD), F32),
        V((T * C, tile, HD), F32), V((T * C, tile, HD), BF16), V((T * C, tile, HD), BF16), V((out_rows, HD), F32),
        dma((4 + 2 * SEQS,)), [dma((2, 2)), dma((2, Y - 1)), dma((2, Y - 1))], dma((2, 2, Y)),
        [dma((2, 2)), dma((2, Y - 1)), dma((2, Y - 1))], dma((2,)), dma((2, Y, C)), dma((2, 2)), dma((2,)),
    ]
    out = pl.pallas_call(
        functools.partial(kernel, sizes),
        out_shape=jax.ShapeDtypeStruct((out_rows, HD), BF16),
        in_specs=[pl.BlockSpec(memory_space=pltpu.HBM)] * 6,
        out_specs=pl.BlockSpec(memory_space=pltpu.VMEM),
        scratch_shapes=scratch,
        compiler_params=pltpu.CompilerParams(
            collective_id=0, has_side_effects=True, vmem_limit_bytes=64 * 1024 * 1024
        ),
        cost_estimate=pl.CostEstimate(
            flops=4 * SEQS * Y * rows * S * HD, bytes_accessed=4 * SEQS * S * HD,
            transcendentals=SEQS * Y * rows * S,
        ),
    )(
        queries.reshape(SEQS, HEADS * HD), keys, values,
        new_keys.reshape(SEQS, HD), new_values.reshape(SEQS, HD), weight,
    )
    return out.reshape(SEQS, Y * C, HD)


def solution(mesh):
    Z = mesh.shape["tp"]
    sizes = (Z, mesh.shape["ctx"] // (2 * Z), 2, mesh.shape["tp"])
    spec = P(None, "ctx", "tp")
    return jax.shard_map(
        functools.partial(build, sizes),
        mesh=mesh,
        in_specs=(spec, spec, spec, spec, spec, P("tp", "ctx")),
        out_specs=P(None, "tp", "ctx"),
        check_vma=False,
    )
```

time: 1250 us -> 69.5 us (0.06)
  the two profiles are of different devices: /device:TPU:7 before, /device:TPU:1 now
where the time goes in v1:
time: 69.5 us; the launch traced here: 69.2 us
  Pallas kernels  67.9 us (98%)
  local copies, waits for them, and re-layouts  1.3 us (2%)
    pallas_call x1, Pallas kernels, build(): pl.pallas_call(functools.partial(kernel, sizes), out_shape=jax.ShapeDtype...  67.9 us

profile of v1, /device:TPU:1, one launch (start us, length us, event | category | flops | bytes accessed | tf_op | source)
XLA Modules:
  0.0 69.2 jit_solution(6327246258191467221)
XLA Ops:
  0.0 67.9 %shard_map.64 = bf16[32,128]{1,0:T(8,128)(2,1)} custom-call(bf16[4,1024]{1,0:T(4,128)(2,1)} %bitcast.5, bf16[4,2048,128]{2,1,0:T(8,128)(2,1)} %k_hbm.1, bf16[4,2048,128]{2,1,0:T(8,128)(2,1)} %v_hbm.1, bf16[4,128]{1,0:T(4,128)(2,1)} %bitcast.6, bf16[4,128]{1,0:T(4,128)(2,1)} %bitcast.7, bf16[1024,128]{1,0:T(8,128)(2,1)} %w_hbm.1), custom_call_target="tpu_custom_call" | custom-call | flops 2147483648 | bytes 4194304 | tf_op jit(solution)/shard_map/pallas_call | solution.py:446
  67.9 1.3 %copy.8 = bf16[4,8,128]{2,1,0:T(8,128)(2,1)} copy(bf16[4,8,128]{2,1,0:T(8,128)(2,1)} %bitcast.4) | data formatting | bytes 16384

commit v2 on v1

--- a/solution.py
+++ b/solution.py
@@ -63,6 +63,9 @@
         self.z = ctx // (self.C * self.Y)
         self.ctx = ctx
         self.tp = lax.axis_index("tp")
+        self.X = self.T // 2
+        self.x = self.tp // 2
+        self.hi = lax.rem(self.tp, 2)
 
     def z_at(self, k):
         return lax.rem(self.z + k + self.Z, self.Z)
@@ -70,8 +73,8 @@
     def y_at(self, k):
         return lax.rem(self.y + k + self.Y, self.Y)
 
-    def tp_at(self, k):
-        return lax.rem(self.tp + k + self.T, self.T)
+    def x_at(self, k):
+        return lax.rem(self.x + k + self.X, self.X)
 
     def ctx_of(self, z, y, c):
         return (z * self.Y + y) * self.C + c
@@ -114,9 +117,11 @@
         loop(0, H, lambda j: self.z_copy((1 - self.half) * H + lax.rem(self.p.z + j, H), 1).start())
         loop(1, H, lambda j: self.z_copy(self.half * H + lax.rem(self.p.z + j, H), 0).start())
 
-    def along_y(self, group, order):
+    def z_arrived(self, group):
         if self.H - 1 + group:
             self.z_all(group).wait_recv()
+
+    def along_y(self, group, order):
         for k in order:
             self.y_copy(k, group, True).start()
 
@@ -124,9 +129,9 @@
         for group in range(2):
             self.y_copy(k, group, False).wait_recv()
 
-    def drain(self):
+    def drain(self, z_too):
         for group in range(2):
-            if self.H - 1 + group:
+            if z_too and self.H - 1 + group:
                 self.z_all(group).wait_send()
             for k in range(1, self.p.Y):
                 self.y_copy(k, group, True).wait_send()
@@ -134,8 +139,8 @@
 
 def kernel(sizes, q_hbm, k_hbm, v_hbm, nk_hbm, nv_hbm, w_hbm, o_ref,
            kbuf, vbuf, vt, wbuf, qin, nkin, nvin, nkb, nvb, qrow, qbuf, qd, sbuf, pbuf, nb, st,
-           ysb, yrb, zf, zsb, zss, zrb, zrs, abuf, af, pf, tf, ts, tr, of,
-           ld, qsems, csems, asems, wsem, ry, rz, tt):
+           ysb, yrb, zsb, zss, zrb, zrs, abuf, af, pf, tf, ts, tr, us, ur, of,
+           ld, qsems, csems, asems, wsem, ry, rz, az, tt, uu):
     p = Place(sizes)
     Z, Y, C, T = sizes
     z, y, c = p.z, p.y, p.c
@@ -161,16 +166,15 @@
     def greet(**axis):
         pl.semaphore_signal(barrier, inc=1, device_id=axis, device_id_type=MESH)
 
-    def greet_tp(k):
-        for cc in range(C):
-            greet(ctx=p.ctx_of(z, y, cc), tp=p.tp_at(k))
-
     loop(1, Z, lambda k: greet(ctx=p.ctx_of(p.z_at(k), y, c)))
     for k in range(1, Y):
         for cc in range(C):
             greet(ctx=p.ctx_of(z, p.y_at(k), cc))
     greet(ctx=p.ctx_of(z, y, 1 - c))
-    loop(1, T, greet_tp)
+    for k in range(1, p.X):
+        greet(tp=p.x_at(k) * 2 + p.hi)
+    for cc in range(C):
+        greet(ctx=p.ctx_of(z, y, cc), tp=p.x * 2 + 1 - p.hi)
     for copy in [kv_load(s)[i] for i in (1, 0) for s in range(SEQS)]:
         copy.start()
     w_load.start()
@@ -184,7 +188,7 @@
     qbuf[y, c, z] = qrow[...].astype(BF16)
     qg = Gather(p, lambda yy: qbuf.at[yy, c], qsems)
     ag = Gather(p, lambda yy: abuf.at[yy], asems)
-    pl.semaphore_wait(barrier, (Z - 1) + (Y * C - 1) + (T - 1) * C)
+    pl.semaphore_wait(barrier, (Z - 1) + (Y * C - 1) + (p.X - 1) + C)
     qg.start()
     nk, nv = nkin[...].astype(F32), nvin[...].astype(F32)
     for s in range(SEQS):
@@ -275,23 +279,37 @@
         dev = p.ctx_of(z, p.y_at(-k), core_at(j))
         return p.copy(ysb.at[k, j], yrb.at[k, j], ry.at[0, k, j], ry.at[1, k, j], ctx=dev)
 
-    def z_copies(k):
-        to = p.z_at(k)
-        dev = p.ctx_of(to, y, c)
-        return (p.copy(zsb.at[to], zrb.at[k - 1], rz.at[0, 0], rz.at[1, 0], ctx=dev),
-                p.copy(zss.at[to], zrs.at[k - 1], rz.at[0, 1], rz.at[1, 1], ctx=dev))
-
-    def z_all():
-        dev = p.ctx_of(p.z_at(1), y, c)
-        return (p.copy(zrb, zrb, rz.at[0, 0], rz.at[1, 0], ctx=dev), p.copy(zrs, zrs, rz.at[0, 1], rz.at[1, 1], ctx=dev))
-
-    def t_copy(k, j):
-        to = p.tp_at(k)
-        return p.copy(ts.at[to * C + core_at(j)], tr.at[k * C + j], tt.at[0], tt.at[1], ctx=p.ctx_of(z, y, core_at(j)), tp=to)
-
-    def t_all():
-        block = tr.at[pl.ds(1, T * C - 1)]
-        return p.copy(block, block, tt.at[0], tt.at[1], ctx=p.ctx_of(z, y, 1 - c))
+    owners = Z // 2
+    mine = z - Z // 4
+    owner = (mine >= 0) & (mine < owners)
+
+    def z_copies(o, index):
+        dev = p.ctx_of(Z // 4 + o, y, c)
+        at = pl.ds(2 * o, 2)
+        return (p.copy(zsb.at[at], zrb.at[index], rz.at[0, 0, o], rz.at[1, 0, index], ctx=dev),
+                p.copy(zss.at[at], zrs.at[index], rz.at[0, 1, o], rz.at[1, 1, index], ctx=dev))
+
+    def others(last, here, body):
+        def one(i):
+            @pl.when(i != here)
+            def _():
+                body(i)
+        loop(0, last, one)
+
+    def a_copy(to, o):
+        block = abuf.at[y, pl.ds(2 * o, 2)]
+        return p.copy(block, block, az.at[0, to], az.at[1, o], ctx=p.ctx_of(to, y, c))
+
+    def t_copy(k):
+        to = p.x_at(k)
+        return p.copy(ts.at[to], tr.at[k - 1], tt.at[0, k - 1], tt.at[1, k - 1], tp=to * 2 + p.hi)
+
+    def u_copy(dh, dc):
+        hi, cc = (1 - p.hi if dh else p.hi), core_at(dc)
+        i = dh * C + dc
+        return p.copy(us.at[hi * C + cc], ur.at[i], uu.at[0, i], uu.at[1, i], ctx=p.ctx_of(z, y, cc), tp=p.x * 2 + hi)
+
+    corners = [(1, 0), (1, 1), (0, 1)]
 
     def message(stats, numer):
         pad = jnp.concatenate([stats, jnp.zeros((PAD - Z, HD), F32)], axis=0)
@@ -321,21 +339,24 @@
         for k in range(Z):
             zss[k] = stats[k:k + 1]
 
-        def send(k):
-            for copy in z_copies(k):
+        def send(o):
+            for copy in z_copies(o, z):
                 copy.start()
-        loop(1, Z, send)
-        zf[...] = numer
+        others(owners, mine, send)
 
     def attended():
-        stats, numers = [zss[z]], [zf[z][None]]
-        for copy in z_all():
-            copy.wait_recv()
-        for k in range(Z - 1):
-            stats.append(zrs[k])
-            numers.append(zrb[k].astype(F32)[None])
-        peak, total, numer = merge(stats, numers)
-        abuf[y, z] = (numer / spread(total, 64))[0].astype(BF16)
+        at = pl.ds(2 * mine, 2)
+        zrb[z] = zsb[at]
+        zrs[z] = zss[at]
+
+        def wait(i):
+            for copy in z_copies(mine, i):
+                copy.wait_recv()
+        others(Z, z, wait)
+        stats = [jnp.concatenate([zrs[i, 0], zrs[i, 1]], axis=0) for i in range(Z)]
+        peak, total, numer = merge(stats, [zrb[i].astype(F32) for i in range(Z)])
+        abuf[y, at] = (numer / spread(total, 64)).astype(BF16)
+        others(Z, z, lambda to: a_copy(to, mine).start())
 
     def project(k):
         block = p.y_at(-k)
@@ -349,8 +370,9 @@
 
     loop(0, SEQS // 2, transpose)
     for group in range(2):
+        qg.z_arrived(group)
+        c_copy(0, group, True).start()
         qg.along_y(group, units)
-        c_copy(0, group, True).start()
     w_load.wait()
     w_copy().start()
     loop(SEQS // 2, SEQS, transpose)
@@ -372,10 +394,15 @@
 
     loop(0, Y, unit)
     reduce_z()
-    attended()
-    ag.start()
+    pl.when(owner)(attended)
     w_copy().wait_recv()
     for group in range(2):
+        for o in range(owners // 2):
+            at = ag.half_at(group) * (owners // 2) + o
+
+            @pl.when(at != mine)
+            def _():
+                a_copy(z, at).wait_recv()
         ag.along_y(group, units)
     for k in [0] + near:
         if k:
@@ -385,27 +412,32 @@
         for cc in range(C):
             tile = [pf[cc, pl.ds(SEQS * t + s, Y, stride=SEQS * Z), :] for s in range(SEQS)]
             tile = jnp.concatenate(tile, axis=0)
-            tf[t * C + cc] = tile
-            ts[t * C + cc] = tile.astype(BF16)
-
-    def send(k):
-        for j in range(C):
-            t_copy(k, j).start()
-
-    loop(1, T, send)
-    t_copy(0, 1).start()
-    mine = tf[p.tp * C + c]
-    t_all().wait_recv()
-    for k in range(1, T):
-        mine = mine + tr[k * C].astype(F32)
-    other = sum(tr[k * C + 1].astype(F32) for k in range(T))
+            tf[t // 2, t % 2 * C + cc] = tile
+            ts[t // 2, t % 2 * C + cc] = tile.astype(BF16)
+    for k in range(1, p.X):
+        t_copy(k).start()
+    total = tf[p.x]
+    for k in range(1, p.X):
+        t_copy(k).wait_recv()
+        total = total + tr[k - 1].astype(F32)
+    tf[p.x] = total
+    us[...] = total.astype(BF16)
+    for corner in corners:
+        u_copy(*corner).start()
+    same = tf[p.x, p.hi * C + c]
+    u_copy(0, 1).wait_recv()
+    other = ur[1].astype(F32)
+    u_copy(1, 0).wait_recv()
+    same = same + ur[C].astype(F32)
+    u_copy(1, 1).wait_recv()
+    other = other + ur[C + 1].astype(F32)
     for s in range(SEQS):
-        of[pl.ds(s * Y * C + c, Y, stride=C), :] = mine[s * Y:(s + 1) * Y]
+        of[pl.ds(s * Y * C + c, Y, stride=C), :] = same[s * Y:(s + 1) * Y]
         of[pl.ds(s * Y * C + 1 - c, Y, stride=C), :] = other[s * Y:(s + 1) * Y]
     o_ref[...] = of[...].astype(BF16)
 
-    qg.drain()
-    ag.drain()
+    qg.drain(True)
+    ag.drain(False)
     w_copy().wait_send()
     for k in range(Y):
         for group in range(2):
@@ -413,9 +445,20 @@
         for j in range(C):
             if k + j:
                 y_copy(k, j).wait_send()
-    for copy in z_all():
-        copy.wait_send()
-    t_all().wait_send()
+
+    def sent(o):
+        for copy in z_copies(o, z):
+            copy.wait_send()
+    others(owners, mine, sent)
+
+    @pl.when(owner)
+    def _():
+        others(Z, z, lambda to: a_copy(to, mine).wait_send())
+
+    for k in range(1, p.X):
+        t_copy(k).wait_send()
+    for corner in corners:
+        u_copy(*corner).wait_send()
 
 
 def build(sizes, queries, keys, values, new_keys, new_values, weight):
@@ -428,6 +471,7 @@
     out_rows = SEQS * Y * C
     block = Z * UNIT + PAD
     tile = SEQS * Y
+    X = T // 2
     scratch = [
         V((SEQS, S, HD), BF16), V((SEQS, S, HD), BF16), V((SEQS // 2, 2 * HD + PAD, S), BF16), V((C,) + weight.shape, BF16),
         V((SEQS, HEADS * HD), BF16), V((SEQS, HD), BF16), V((SEQS, HD), BF16),
@@ -436,12 +480,14 @@
         V((SEQS // 2, S, 2 * rows), F32), V((SEQS // 2, S, 2 * rows), BF16),
         V((Y, C, Z, UNIT, HD), F32), V((Y, C, Z, HD), F32),
         V((Y, C, block, HD), BF16), V((Y, C, block, HD), BF16),
-        V((Z, UNIT, HD), F32), V((Z, UNIT, HD), BF16), V((Z, 1, HD), F32),
-        V((Z - 1, UNIT, HD), BF16), V((Z - 1, 1, HD), F32),
+        V((Z, UNIT, HD), BF16), V((Z, 1, HD), F32),
+        V((Z, 2, UNIT, HD), BF16), V((Z, 2, 1, HD), F32),
         V((Y, Z, UNIT, HD), BF16), V((Z * UNIT, HD), F32), V((C, Y * Z * SEQS, HD), F32),
-        V((T * C, tile, HD), F32), V((T * C, tile, HD), BF16), V((T * C, tile, HD), BF16), V((out_rows, HD), F32),
+        V((X, 2 * C, tile, HD), F32), V((X, 2 * C, tile, HD), BF16), V((max(X - 1, 1), 2 * C, tile, HD), BF16),
+        V((2 * C, tile, HD), BF16), V((2 * C, tile, HD), BF16), V((out_rows, HD), F32),
         dma((4 + 2 * SEQS,)), [dma((2, 2)), dma((2, Y - 1)), dma((2, Y - 1))], dma((2, 2, Y)),
-        [dma((2, 2)), dma((2, Y - 1)), dma((2, Y - 1))], dma((2,)), dma((2, Y, C)), dma((2, 2)), dma((2,)),
+        [dma((2, 2)), dma((2, Y - 1)), dma((2, Y - 1))], dma((2,)), dma((2, Y, C)),
+        dma((2, 2, Z)), dma((2, Z)), dma((2, max(X - 1, 1))), dma((2, 2 * C)),
     ]
     out = pl.pallas_call(
         functools.partial(kernel, sizes),

time: 69.5 us -> 70.5 us (1.014)
  Pallas kernels: 67.9 us -> 69 us
    pallas_call x1, Pallas kernels: 67.9 us -> 69 us  [build(): pl.pallas_call(functools.partial(kernel, sizes), out_shape=jax.ShapeDtype...]
where the time goes in v2:
time: 70.5 us; the launch traced here: 70.3 us
  Pallas kernels  69 us (98%)
  local copies, waits for them, and re-layouts  1.3 us (2%)
    pallas_call x1, Pallas kernels, build(): pl.pallas_call(functools.partial(kernel, sizes), out_shape=jax.ShapeDtype...  69 us

profile of v2, /device:TPU:1, one launch (start us, length us, event | category | flops | bytes accessed | tf_op | source)
XLA Modules:
  0.0 70.3 jit_solution(11833114585487468996)
XLA Ops:
  0.0 69.0 %shard_map.64 = bf16[32,128]{1,0:T(8,128)(2,1)} custom-call(bf16[4,1024]{1,0:T(4,128)(2,1)} %bitcast.5, bf16[4,2048,128]{2,1,0:T(8,128)(2,1)} %k_hbm.1, bf16[4,2048,128]{2,1,0:T(8,128)(2,1)} %v_hbm.1, bf16[4,128]{1,0:T(4,128)(2,1)} %bitcast.6, bf16[4,128]{1,0:T(4,128)(2,1)} %bitcast.7, bf16[1024,128]{1,0:T(8,128)(2,1)} %w_hbm.1), custom_call_target="tpu_custom_call" | custom-call | flops 2147483648 | bytes 4194304 | tf_op jit(solution)/shard_map/pallas_call | solution.py:492
  69.0 1.3 %copy.8 = bf16[4,8,128]{2,1,0:T(8,128)(2,1)} copy(bf16[4,8,128]{2,1,0:T(8,128)(2,1)} %bitcast.4) | data formatting | bytes 16384

commit v3 on v2

--- a/solution.py
+++ b/solution.py
@@ -63,9 +63,6 @@
         self.z = ctx // (self.C * self.Y)
         self.ctx = ctx
         self.tp = lax.axis_index("tp")
-        self.X = self.T // 2
-        self.x = self.tp // 2
-        self.hi = lax.rem(self.tp, 2)
 
     def z_at(self, k):
         return lax.rem(self.z + k + self.Z, self.Z)
@@ -73,8 +70,8 @@
     def y_at(self, k):
         return lax.rem(self.y + k + self.Y, self.Y)
 
-    def x_at(self, k):
-        return lax.rem(self.x + k + self.X, self.X)
+    def tp_at(self, k):
+        return lax.rem(self.tp + k + self.T, self.T)
 
     def ctx_of(self, z, y, c):
         return (z * self.Y + y) * self.C + c
@@ -139,8 +136,8 @@
 
 def kernel(sizes, q_hbm, k_hbm, v_hbm, nk_hbm, nv_hbm, w_hbm, o_ref,
            kbuf, vbuf, vt, wbuf, qin, nkin, nvin, nkb, nvb, qrow, qbuf, qd, sbuf, pbuf, nb, st,
-           ysb, yrb, zsb, zss, zrb, zrs, abuf, af, pf, tf, ts, tr, us, ur, of,
-           ld, qsems, csems, asems, wsem, ry, rz, az, tt, uu):
+           ysb, yrb, zsb, zss, zrb, zrs, abuf, af, pf, tf, ts, tr, of,
+           ld, qsems, csems, asems, wsem, ry, rz, az, tt):
     p = Place(sizes)
     Z, Y, C, T = sizes
     z, y, c = p.z, p.y, p.c
@@ -171,10 +168,11 @@
         for cc in range(C):
             greet(ctx=p.ctx_of(z, p.y_at(k), cc))
     greet(ctx=p.ctx_of(z, y, 1 - c))
-    for k in range(1, p.X):
-        greet(tp=p.x_at(k) * 2 + p.hi)
-    for cc in range(C):
-        greet(ctx=p.ctx_of(z, y, cc), tp=p.x * 2 + 1 - p.hi)
+    def greet_tp(k):
+        for cc in range(C):
+            greet(ctx=p.ctx_of(z, y, cc), tp=p.tp_at(k))
+
+    loop(1, T, greet_tp)
     for copy in [kv_load(s)[i] for i in (1, 0) for s in range(SEQS)]:
         copy.start()
     w_load.start()
@@ -188,7 +186,7 @@
     qbuf[y, c, z] = qrow[...].astype(BF16)
     qg = Gather(p, lambda yy: qbuf.at[yy, c], qsems)
     ag = Gather(p, lambda yy: abuf.at[yy], asems)
-    pl.semaphore_wait(barrier, (Z - 1) + (Y * C - 1) + (p.X - 1) + C)
+    pl.semaphore_wait(barrier, (Z - 1) + (Y * C - 1) + (T - 1) * C)
     qg.start()
     nk, nv = nkin[...].astype(F32), nvin[...].astype(F32)
     for s in range(SEQS):
@@ -300,16 +298,13 @@
         block = abuf.at[y, pl.ds(2 * o, 2)]
         return p.copy(block, block, az.at[0, to], az.at[1, o], ctx=p.ctx_of(to, y, c))
 
-    def t_copy(k):
-        to = p.x_at(k)
-        return p.copy(ts.at[to], tr.at[k - 1], tt.at[0, k - 1], tt.at[1, k - 1], tp=to * 2 + p.hi)
-
-    def u_copy(dh, dc):
-        hi, cc = (1 - p.hi if dh else p.hi), core_at(dc)
-        i = dh * C + dc
-        return p.copy(us.at[hi * C + cc], ur.at[i], uu.at[0, i], uu.at[1, i], ctx=p.ctx_of(z, y, cc), tp=p.x * 2 + hi)
-
-    corners = [(1, 0), (1, 1), (0, 1)]
+    def t_copy(k, j):
+        to = p.tp_at(k)
+        return p.copy(ts.at[to * C + core_at(j)], tr.at[k * C + j], tt.at[0], tt.at[1], ctx=p.ctx_of(z, y, core_at(j)), tp=to)
+
+    def t_all():
+        block = tr.at[pl.ds(1, T * C - 1)]
+        return p.copy(block, block, tt.at[0], tt.at[1], ctx=p.ctx_of(z, y, 1 - c))
 
     def message(stats, numer):
         pad = jnp.concatenate([stats, jnp.zeros((PAD - Z, HD), F32)], axis=0)
@@ -358,15 +353,32 @@
         abuf[y, at] = (numer / spread(total, 64)).astype(BF16)
         others(Z, z, lambda to: a_copy(to, mine).start())
 
-    def project(k):
-        block = p.y_at(-k)
-        af[...] = abuf[block].reshape(Z * UNIT, HD).astype(F32)
-        n = Z * SEQS
+    def project(group):
+        for k in near:
+            ag.y_copy(k, group, False).wait_recv()
+        H = Z // 2
+        n = Y * H * SEQS
+        af[...] = abuf[:, ag.rows(group)].reshape(n * HEADS, HD).astype(F32)
         heads = [af[pl.ds(hd, n, stride=HEADS), :].astype(BF16) for hd in range(HEADS)]
-        at = pl.multiple_of(block * n, n)
         both = jnp.dot(jnp.concatenate(heads, axis=1), jnp.concatenate([wbuf[0], wbuf[1]], axis=1), preferred_element_type=F32)
         for cc in range(C):
-            pf[cc, pl.ds(at, n), :] = both[:, cc * HD:(cc + 1) * HD]
+            pf[group, cc] = both[:, cc * HD:(cc + 1) * HD]
+        for zz in range(H):
+            t = ag.half_at(group) * H + zz
+            for cc in range(C):
+                tile = [pf[group, cc, pl.ds(SEQS * zz + s, Y, stride=SEQS * H), :] for s in range(SEQS)]
+                tile = jnp.concatenate(tile, axis=0)
+                tf[t * C + cc] = tile
+                ts[t * C + cc] = tile.astype(BF16)
+
+        def send(zz):
+            k = lax.rem(ag.half_at(group) * H + zz - p.tp + T, T)
+
+            @pl.when(k > 0)
+            def _():
+                t_copy(k, 0).start()
+            t_copy(k, 1).start()
+        loop(0, H, send)
 
     loop(0, SEQS // 2, transpose)
     for group in range(2):
@@ -404,33 +416,13 @@
             def _():
                 a_copy(z, at).wait_recv()
         ag.along_y(group, units)
-    for k in [0] + near:
-        if k:
-            ag.arrived(k)
-        project(k)
-    for t in range(T):
-        for cc in range(C):
-            tile = [pf[cc, pl.ds(SEQS * t + s, Y, stride=SEQS * Z), :] for s in range(SEQS)]
-            tile = jnp.concatenate(tile, axis=0)
-            tf[t // 2, t % 2 * C + cc] = tile
-            ts[t // 2, t % 2 * C + cc] = tile.astype(BF16)
-    for k in range(1, p.X):
-        t_copy(k).start()
-    total = tf[p.x]
-    for k in range(1, p.X):
-        t_copy(k).wait_recv()
-        total = total + tr[k - 1].astype(F32)
-    tf[p.x] = total
-    us[...] = total.astype(BF16)
-    for corner in corners:
-        u_copy(*corner).start()
-    same = tf[p.x, p.hi * C + c]
-    u_copy(0, 1).wait_recv()
-    other = ur[1].astype(F32)
-    u_copy(1, 0).wait_recv()
-    same = same + ur[C].astype(F32)
-    u_copy(1, 1).wait_recv()
-    other = other + ur[C + 1].astype(F32)
+    for group in range(2):
+        project(group)
+    same = tf[p.tp * C + c]
+    t_all().wait_recv()
+    for k in range(1, T):
+        same = same + tr[k * C].astype(F32)
+    other = sum(tr[k * C + 1].astype(F32) for k in range(T))
     for s in range(SEQS):
         of[pl.ds(s * Y * C + c, Y, stride=C), :] = same[s * Y:(s + 1) * Y]
         of[pl.ds(s * Y * C + 1 - c, Y, stride=C), :] = other[s * Y:(s + 1) * Y]
@@ -455,10 +447,7 @@
     def _():
         others(Z, z, lambda to: a_copy(to, mine).wait_send())
 
-    for k in range(1, p.X):
-        t_copy(k).wait_send()
-    for corner in corners:
-        u_copy(*corner).wait_send()
+    t_all().wait_send()
 
 
 def build(sizes, queries, keys, values, new_keys, new_values, weight):
@@ -471,7 +460,6 @@
     out_rows = SEQS * Y * C
     block = Z * UNIT + PAD
     tile = SEQS * Y
-    X = T // 2
     scratch = [
         V((SEQS, S, HD), BF16), V((SEQS, S, HD), BF16), V((SEQS // 2, 2 * HD + PAD, S), BF16), V((C,) + weight.shape, BF16),
         V((SEQS, HEADS * HD), BF16), V((SEQS, HD), BF16), V((SEQS, HD), BF16),
@@ -482,12 +470,11 @@
         V((Y, C, block, HD), BF16), V((Y, C, block, HD), BF16),
         V((Z, UNIT, HD), BF16), V((Z, 1, HD), F32),
         V((Z, 2, UNIT, HD), BF16), V((Z, 2, 1, HD), F32),
-        V((Y, Z, UNIT, HD), BF16), V((Z * UNIT, HD), F32), V((C, Y * Z * SEQS, HD), F32),
-        V((X, 2 * C, tile, HD), F32), V((X, 2 * C, tile, HD), BF16), V((max(X - 1, 1), 2 * C, tile, HD), BF16),
-        V((2 * C, tile, HD), BF16), V((2 * C, tile, HD), BF16), V((out_rows, HD), F32),
+        V((Y, Z, UNIT, HD), BF16), V((Y * Z // 2 * UNIT, HD), F32), V((2, C, Y * Z // 2 * SEQS, HD), F32),
+        V((T * C, tile, HD), F32), V((T * C, tile, HD), BF16), V((T * C, tile, HD), BF16), V((out_rows, HD), F32),
         dma((4 + 2 * SEQS,)), [dma((2, 2)), dma((2, Y - 1)), dma((2, Y - 1))], dma((2, 2, Y)),
         [dma((2, 2)), dma((2, Y - 1)), dma((2, Y - 1))], dma((2,)), dma((2, Y, C)),
-        dma((2, 2, Z)), dma((2, Z)), dma((2, max(X - 1, 1))), dma((2, 2 * C)),
+        dma((2, 2, Z)), dma((2, Z)), dma((2,)),
     ]
     out = pl.pallas_call(
         functools.partial(kernel, sizes),

time: 70.5 us -> 67.1 us (0.952)
  the two profiles are of different devices: /device:TPU:1 before, /device:TPU:7 now
where the time goes in v3:
time: 67.1 us; the launch traced here: 66.9 us
  Pallas kernels  65.5 us (98%)
  local copies, waits for them, and re-layouts  1.3 us (2%)
    pallas_call x1, Pallas kernels, build(): pl.pallas_call(functools.partial(kernel, sizes), out_shape=jax.ShapeDtype...  65.5 us

profile of v3, /device:TPU:7, one launch (start us, length us, event | category | flops | bytes accessed | tf_op | source)
XLA Modules:
  0.0 66.9 jit_solution(8009456633649501945)
XLA Ops:
  0.0 65.5 %shard_map.64 = bf16[32,128]{1,0:T(8,128)(2,1)} custom-call(bf16[4,1024]{1,0:T(4,128)(2,1)} %bitcast.5, bf16[4,2048,128]{2,1,0:T(8,128)(2,1)} %k_hbm.1, bf16[4,2048,128]{2,1,0:T(8,128)(2,1)} %v_hbm.1, bf16[4,128]{1,0:T(4,128)(2,1)} %bitcast.6, bf16[4,128]{1,0:T(4,128)(2,1)} %bitcast.7, bf16[1024,128]{1,0:T(8,128)(2,1)} %w_hbm.1), custom_call_target="tpu_custom_call" | custom-call | flops 2147483648 | bytes 4194304 | tf_op jit(solution)/shard_map/pallas_call | solution.py:479
  65.6 1.3 %copy.8 = bf16[4,8,128]{2,1,0:T(8,128)(2,1)} copy(bf16[4,8,128]{2,1,0:T(8,128)(2,1)} %bitcast.4) | data formatting | bytes 16384

commit v4 on v3

--- a/solution.py
+++ b/solution.py
@@ -13,7 +13,7 @@
 SEQS = 4
 UNIT = SEQS * HEADS
 PAD = 16
-CHUNK = 256
+CHUNK = 128
 SCALE = math.log2(math.e) / math.sqrt(HD)
 MESH = pl.DeviceIdType.MESH
 F32 = jnp.float32

time: 67.1 us -> 67 us (level)
  no operation moved by 1% of the time
where the time goes in v4:
time: 67 us; the launch traced here: 66.8 us
  Pallas kernels  65.5 us (98%)
  local copies, waits for them, and re-layouts  1.3 us (2%)
    pallas_call x1, Pallas kernels, build(): pl.pallas_call(functools.partial(kernel, sizes), out_shape=jax.ShapeDtype...  65.5 us

profile of v4, /device:TPU:7, one launch (start us, length us, event | category | flops | bytes accessed | tf_op | source)
XLA Modules:
  0.0 66.8 jit_solution(2976032485499433415)
XLA Ops:
  0.0 65.5 %shard_map.64 = bf16[32,128]{1,0:T(8,128)(2,1)} custom-call(bf16[4,1024]{1,0:T(4,128)(2,1)} %bitcast.5, bf16[4,2048,128]{2,1,0:T(8,128)(2,1)} %k_hbm.1, bf16[4,2048,128]{2,1,0:T(8,128)(2,1)} %v_hbm.1, bf16[4,128]{1,0:T(4,128)(2,1)} %bitcast.6, bf16[4,128]{1,0:T(4,128)(2,1)} %bitcast.7, bf16[1024,128]{1,0:T(8,128)(2,1)} %w_hbm.1), custom_call_target="tpu_custom_call" | custom-call | flops 2147483648 | bytes 4194304 | tf_op jit(solution)/shard_map/pallas_call | solution.py:479
  65.5 1.3 %copy.8 = bf16[4,8,128]{2,1,0:T(8,128)(2,1)} copy(bf16[4,8,128]{2,1,0:T(8,128)(2,1)} %bitcast.4) | data formatting | bytes 16384

commit v5 on v3

--- a/solution.py
+++ b/solution.py
@@ -351,7 +351,14 @@
         stats = [jnp.concatenate([zrs[i, 0], zrs[i, 1]], axis=0) for i in range(Z)]
         peak, total, numer = merge(stats, [zrb[i].astype(F32) for i in range(Z)])
         abuf[y, at] = (numer / spread(total, 64)).astype(BF16)
-        others(Z, z, lambda to: a_copy(to, mine).start())
+
+        def send(j):
+            to = lax.rem(z + Z // 2 + j, Z)
+
+            @pl.when(to != z)
+            def _():
+                a_copy(to, mine).start()
+        loop(0, Z, send)
 
     def project(group):
         for k in near:

time: 67.1 us -> 67.6 us (level)
  no operation moved by 1% of the time
where the time goes in v5:
time: 67.6 us; the launch traced here: 67.4 us
  Pallas kernels  66.1 us (98%)
  local copies, waits for them, and re-layouts  1.3 us (2%)
    pallas_call x1, Pallas kernels, build(): pl.pallas_call(functools.partial(kernel, sizes), out_shape=jax.ShapeDtype...  66.1 us

profile of v5, /device:TPU:7, one launch (start us, length us, event | category | flops | bytes accessed | tf_op | source)
XLA Modules:
  0.0 67.4 jit_solution(17153213750913325919)
XLA Ops:
  0.0 66.1 %shard_map.64 = bf16[32,128]{1,0:T(8,128)(2,1)} custom-call(bf16[4,1024]{1,0:T(4,128)(2,1)} %bitcast.5, bf16[4,2048,128]{2,1,0:T(8,128)(2,1)} %k_hbm.1, bf16[4,2048,128]{2,1,0:T(8,128)(2,1)} %v_hbm.1, bf16[4,128]{1,0:T(4,128)(2,1)} %bitcast.6, bf16[4,128]{1,0:T(4,128)(2,1)} %bitcast.7, bf16[1024,128]{1,0:T(8,128)(2,1)} %w_hbm.1), custom_call_target="tpu_custom_call" | custom-call | flops 2147483648 | bytes 4194304 | tf_op jit(solution)/shard_map/pallas_call | solution.py:486
  66.1 1.3 %copy.8 = bf16[4,8,128]{2,1,0:T(8,128)(2,1)} copy(bf16[4,8,128]{2,1,0:T(8,128)(2,1)} %bitcast.4) | data formatting | bytes 16384
